TPU v7x, 256 devices: a whole 4x4x8 slice. The times are simulated.
256 devices in a mesh: ctx: 64 (over z_hi, y, x), head: 4 (over z_lo, core).
Axes of the slice: x: 4, y: 4, z: 8 (z_hi: 4, z_lo: 2; z = z_hi * 2 + z_lo), core: 2. Of those that a mesh axis runs over, the one named last changes fastest.
Arguments:
- queries: bfloat16 [16384, 4096], P('ctx', 'head'), may hold values from -30 to 30
- keys: bfloat16 [16384, 512], P('ctx', 'head'), may hold values from -30 to 30
- values: bfloat16 [16384, 512], P('ctx', 'head'), may hold values from -6 to 6
- lengths: int32 [32], replicated, may hold values from 1 to 2560, 16384 in all
- output_gradient: bfloat16 [16384, 4096], P('ctx', 'head'), may hold values from -6 to 6
Outputs:
- attn_out: bfloat16 [16384, 4096], P('ctx', 'head')
- query_grad: float32 [16384, 4096], P('ctx', 'head')
- key_grad: float32 [16384, 512], P('ctx', 'head')
- value_grad: float32 [16384, 512], P('ctx', 'head')
Inputs may be any that keep to these rules, and one draw needn't show every extreme that they name: `lengths`: the documents fill the 16384 tokens in order; the longest has exactly 2560 tokens.
All inputs are finite; a program needn't handle non-finite values.
Results may differ from a plain program's by a relative error of at most 0.013.
Values may be sent and summed in bfloat16 or wider, within the bound.
A program may use at most 64 MiB of HBM per device.

v0:
```python
import jax
import jax.numpy as jnp
from jax import lax
from jax.sharding import PartitionSpec as P

QUERY_HEADS = 32
KEY_VALUE_HEADS = 4
HEAD_SIZE = 128


neg_big = -1e30


def from_behind(block, axis, distance):
    devices = range(lax.axis_size(axis))
    route = [(i - distance, i) for i in devices if i - distance in devices]
    return lax.ppermute(block, axis, route)


def doc_of(lengths, positions):
    ends = jnp.cumsum(lengths)
    found = jnp.sum((positions[:, None] >= ends[None, :]).astype(jnp.int32), axis=1)
    return jnp.where(positions >= 0, found, -1)


def body(queries, keys, values, lengths, output_gradient):
    tok_rows = queries.shape[0]
    local_kv = keys.shape[1] // HEAD_SIZE
    group_members = QUERY_HEADS // KEY_VALUE_HEADS
    factor = HEAD_SIZE ** (-0.5)
    reach_len = min(10, lax.axis_size("ctx") // 2)
    my_shard = lax.axis_index("ctx")
    paired = jnp.stack([keys, values])
    arrived = [paired]
    moving = paired
    for hop_count in range(reach_len):
        moving = from_behind(moving, "ctx", 1)
        arrived.append(moving)
    window = jnp.stack(arrived[::-1])
    offsets = jnp.arange(tok_rows, dtype=jnp.int32)
    q_pos = my_shard * tok_rows + offsets
    q_doc = doc_of(lengths, q_pos)
    q_heads = queries.reshape(tok_rows, local_kv, group_members, HEAD_SIZE)
    g_heads = output_gradient.reshape(tok_rows, local_kv, group_members, HEAD_SIZE)

    def scored(block_no):
        pair_now = lax.dynamic_index_in_dim(window, block_no, 0, keepdims=False)
        current_key = pair_now[0].reshape(tok_rows, local_kv, HEAD_SIZE)
        current_value = pair_now[1].reshape(tok_rows, local_kv, HEAD_SIZE)
        k_pos = (my_shard - reach_len + block_no) * tok_rows + offsets
        k_doc = doc_of(lengths, k_pos)
        allowed = (q_doc[:, None] == k_doc[None, :]) & (k_pos[None, :] <= q_pos[:, None])
        scores = (
            jnp.einsum("tkgd,skd->kgts", q_heads, current_key, preferred_element_type=jnp.float32)
            * factor
        )
        return (current_key, current_value, allowed, jnp.where(allowed, scores, neg_big))

    def first_pass(block_no, carry):
        peak, total = carry
        current_key, current_value, allowed, scores = scored(block_no)
        new_peak = jnp.maximum(peak, jnp.max(scores, axis=-1))
        terms = jnp.where(allowed, jnp.exp(scores - new_peak[..., None]), 0.0)
        return (new_peak, total * jnp.exp(peak - new_peak) + jnp.sum(terms, axis=-1))

    stat_shape = (local_kv, group_members, tok_rows)
    peak, total = lax.fori_loop(
        0,
        reach_len + 1,
        first_pass,
        (jnp.full(stat_shape, neg_big, jnp.float32), jnp.zeros(stat_shape, jnp.float32)),
    )

    def weights(allowed, scores):
        return jnp.where(allowed, jnp.exp(scores - peak[..., None]), 0.0) / total[..., None]

    def second_pass(block_no, acc_out):
        current_key, current_value, allowed, scores = scored(block_no)
        probabilities_reduced = weights(allowed, scores).astype(jnp.bfloat16)
        return acc_out + jnp.einsum(
            "kgts,skd->tkgd",
            probabilities_reduced,
            current_value,
            preferred_element_type=jnp.float32,
        )

    head_shape = (tok_rows, local_kv, group_members, HEAD_SIZE)
    acc_out = lax.fori_loop(0, reach_len + 1, second_pass, jnp.zeros(head_shape, jnp.float32))
    attn_out = acc_out.astype(jnp.bfloat16).reshape(tok_rows, -1)
    delta = jnp.einsum("tkgd,tkgd->kgt", g_heads.astype(jnp.float32), acc_out)

    def third_pass(acc_grad, block_no):
        current_key, current_value, allowed, scores = scored(block_no)
        probs = weights(allowed, scores)
        probabilities_reduced = probs.astype(jnp.bfloat16)
        slope = jnp.einsum(
            "tkgd,skd->kgts", g_heads, current_value, preferred_element_type=jnp.float32
        )
        score_gradient = (probs * (slope - delta[..., None]) * factor).astype(jnp.bfloat16)
        acc_grad = acc_grad + jnp.einsum(
            "kgts,skd->tkgd", score_gradient, current_key, preferred_element_type=jnp.float32
        )
        key_part = jnp.einsum(
            "iofz,fion->zin", score_gradient, q_heads, preferred_element_type=jnp.float32
        )
        value_part = jnp.einsum(
            "iofz,fion->zin", probabilities_reduced, g_heads, preferred_element_type=jnp.float32
        )
        return (
            acc_grad,
            jnp.stack([key_part.reshape(tok_rows, -1), value_part.reshape(tok_rows, -1)]),
        )

    acc_grad, partials = lax.scan(
        third_pass, jnp.zeros(head_shape, jnp.float32), jnp.arange(reach_len + 1, dtype=jnp.int32)
    )
    carried = partials[0]
    for hop_count in range(1, reach_len + 1):
        carried = from_behind(carried, "ctx", -1) + partials[hop_count]
    return (attn_out, acc_grad.reshape(tok_rows, -1), carried[0], carried[1])


def solution(mesh):
    return jax.shard_map(
        body,
        mesh=mesh,
        in_specs=(P("ctx", "head"), P("ctx", "head"), P("ctx", "head"), P(), P("ctx", "head")),
        out_specs=(P("ctx", "head"), P("ctx", "head"), P("ctx", "head"), P("ctx", "head")),
        check_vma=False,
    )
```

profile of v0, /device:TPU:94, one launch (start us, length us, event | category | flops | bytes accessed | tf_op | source)
XLA Modules:
  0.0 471.3 jit_solution(554935296875817553)
XLA Ops:
  1.6 6.0 %collective-permute-start = (bf16[2,256,128]{2,1,0:T(8,128)(2,1)S(1)}, bf16[2,256,128]{2,1,0:T(8,128)(2,1)S(1)}, u32[]{:S(2)}, u32[]{:S(2)}) collective-permute-start(bf16[2,256,128]{2,1,0:T(8,128)(2,1)S(1)} %pad_maximum_fusion), channel_id=1, source_target_pairs={{0,4},{4,8},{8,12},{12,16},{16,20},{20,24},{24,28},{28,32},{32,36}... | collective-permute-start | bytes 393224 | tf_op jit(solution)/shard_map/ppermute | solution.py:17
  7.6 5.4 %collective-permute-done = bf16[2,256,128]{2,1,0:T(8,128)(2,1)S(1)} collective-permute-done((bf16[2,256,128]{2,1,0:T(8,128)(2,1)S(1)}, bf16[2,256,128]{2,1,0:T(8,128)(2,1)S(1)}, u32[]{:S(2)}, u32[]{:S(2)}) %collective-permute-start) | collective-permute-done | bytes 131104 | tf_op jit(solution)/shard_map/ppermute | solution.py:17
  13.0 10.7 %collective-permute-start.1 = (bf16[2,256,128]{2,1,0:T(8,128)(2,1)S(1)}, bf16[2,256,128]{2,1,0:T(8,128)(2,1)S(1)}, u32[]{:S(2)}, u32[]{:S(2)}) collective-permute-start(bf16[2,256,128]{2,1,0:T(8,128)(2,1)S(1)} %collective-permute-done), channel_id=1, source_target_pairs={{0,4},{4,8},{8,12},{12,16},{16,20},{20,24},{24,28},{28,32},{32,36}... | collective-permute-start | bytes 393224 | tf_op jit(solution)/shard_map/ppermute | solution.py:17
  23.7 2.6 collective-permute-done.1
  26.3 10.8 %collective-permute-start.2 = (bf16[2,256,128]{2,1,0:T(8,128)(2,1)S(1)}, bf16[2,256,128]{2,1,0:T(8,128)(2,1)S(1)}, u32[]{:S(2)}, u32[]{:S(2)}) collective-permute-start(bf16[2,256,128]{2,1,0:T(8,128)(2,1)S(1)} %collective-permute-done.1), channel_id=1, source_target_pairs={{0,4},{4,8},{8,12},{12,16},{16,20},{20,24},{24,28},{28,32},{32,36}... | collective-permute-start | bytes 393224 | tf_op jit(solution)/shard_map/ppermute | solution.py:17
  37.1 2.5 collective-permute-done.2
  39.6 10.8 %collective-permute-start.3 = (bf16[2,256,128]{2,1,0:T(8,128)(2,1)S(1)}, bf16[2,256,128]{2,1,0:T(8,128)(2,1)S(1)}, u32[]{:S(2)}, u32[]{:S(2)}) collective-permute-start(bf16[2,256,128]{2,1,0:T(8,128)(2,1)S(1)} %collective-permute-done.2), channel_id=1, source_target_pairs={{0,4},{4,8},{8,12},{12,16},{16,20},{20,24},{24,28},{28,32},{32,36}... | collective-permute-start | bytes 393224 | tf_op jit(solution)/shard_map/ppermute | solution.py:17
  50.4 2.5 collective-permute-done.3
  52.9 10.7 %collective-permute-start.4 = (bf16[2,256,128]{2,1,0:T(8,128)(2,1)S(1)}, bf16[2,256,128]{2,1,0:T(8,128)(2,1)S(1)}, u32[]{:S(2)}, u32[]{:S(2)}) collective-permute-start(bf16[2,256,128]{2,1,0:T(8,128)(2,1)S(1)} %collective-permute-done.3), channel_id=1, source_target_pairs={{0,4},{4,8},{8,12},{12,16},{16,20},{20,24},{24,28},{28,32},{32,36}... | collective-permute-start | bytes 393224 | tf_op jit(solution)/shard_map/ppermute | solution.py:17
  63.5 2.5 collective-permute-done.4
  66.0 10.7 %collective-permute-start.5 = (bf16[2,256,128]{2,1,0:T(8,128)(2,1)S(1)}, bf16[2,256,128]{2,1,0:T(8,128)(2,1)S(1)}, u32[]{:S(2)}, u32[]{:S(2)}) collective-permute-start(bf16[2,256,128]{2,1,0:T(8,128)(2,1)S(1)} %collective-permute-done.4), channel_id=1, source_target_pairs={{0,4},{4,8},{8,12},{12,16},{16,20},{20,24},{24,28},{28,32},{32,36}... | collective-permute-start | bytes 393224 | tf_op jit(solution)/shard_map/ppermute | solution.py:17
  76.7 2.5 collective-permute-done.5
  79.2 10.7 %collective-permute-start.6 = (bf16[2,256,128]{2,1,0:T(8,128)(2,1)S(1)}, bf16[2,256,128]{2,1,0:T(8,128)(2,1)S(1)}, u32[]{:S(2)}, u32[]{:S(2)}) collective-permute-start(bf16[2,256,128]{2,1,0:T(8,128)(2,1)S(1)} %collective-permute-done.5), channel_id=1, source_target_pairs={{0,4},{4,8},{8,12},{12,16},{16,20},{20,24},{24,28},{28,32},{32,36}... | collective-permute-start | bytes 393224 | tf_op jit(solution)/shard_map/ppermute | solution.py:17
  89.9 2.6 collective-permute-done.6
  92.5 10.7 %collective-permute-start.7 = (bf16[2,256,128]{2,1,0:T(8,128)(2,1)S(1)}, bf16[2,256,128]{2,1,0:T(8,128)(2,1)}, u32[]{:S(2)}, u32[]{:S(2)}) collective-permute-start(bf16[2,256,128]{2,1,0:T(8,128)(2,1)S(1)} %collective-permute-done.6), channel_id=1, source_target_pairs={{0,4},{4,8},{8,12},{12,16},{16,20},{20,24},{24,28},{28,32},{32,36}... | collective-permute-start | bytes 393224 | tf_op jit(solution)/shard_map/ppermute | solution.py:17
  103.2 2.5 collective-permute-done.7
  105.7 10.8 %collective-permute-start.8 = (bf16[2,256,128]{2,1,0:T(8,128)(2,1)}, bf16[2,256,128]{2,1,0:T(8,128)(2,1)}, u32[]{:S(2)}, u32[]{:S(2)}) collective-permute-start(bf16[2,256,128]{2,1,0:T(8,128)(2,1)} %collective-permute-done.7), channel_id=1, source_target_pairs={{0,4},{4,8},{8,12},{12,16},{16,20},{20,24},{24,28},{28,32},{32,36}... | collective-permute-start | bytes 393224 | tf_op jit(solution)/shard_map/ppermute | solution.py:17
  117.5 2.0 copy.31
  124.2 9.0 %collective-permute-start.9 = (bf16[2,256,128]{2,1,0:T(8,128)(2,1)}, bf16[2,256,128]{2,1,0:T(8,128)(2,1)S(1)}, u32[]{:S(2)}, u32[]{:S(2)}) collective-permute-start(bf16[2,256,128]{2,1,0:T(8,128)(2,1)} %collective-permute-done.8), channel_id=1, source_target_pairs={{0,4},{4,8},{8,12},{12,16},{16,20},{20,24},{24,28},{28,32},{32,36}... | collective-permute-start | bytes 393224 | tf_op jit(solution)/shard_map/ppermute | solution.py:17
  133.3 2.8 collective-permute-done.9
  143.8 23.7 %while.49 = (s32[]{:T(128)}, f32[1,8,256]{2,1,0:T(8,128)S(1)}, f32[1,8,256]{2,1,0:T(8,128)S(1)}, s32[256]{0:T(256)S(1)}, s32[]{:T(128)}, /*index=5*/s32[1,32]{1,...) while((s32[]{:T(128)}, f32[1,8,256]{2,1,0:T(8,128)S(1)}, ...), condition=%wide.region_6.7_spmd.clone, body=%wide.region_2.6_spmd.clone.sunk | while | flops 138644480 | bytes 5097776 | solution.py:67
  167.5 24.8 %while.50 = (s32[]{:T(128)}, f32[256,1,8,128]{0,3,2,1:T(8,128)S(1)}, bf16[11,2,256,128]{3,2,1,0:T(8,128)(2,1)}, s32[256]{0:T(256)S(1)}, s32[]{:T(128)}, /*index=...) while((s32[]{:T(128)}, ...), condition=%wide.region_9.10_spmd.clone, body=%wide.region_7.9_spmd.clone.sunk | while | flops 272327680 | bytes 2912582 | solution.py:88
  167.8 2.0 fusion.73
  170.0 2.0 fusion.73
  172.3 2.0 fusion.73
  174.5 2.0 fusion.73
  176.8 2.0 fusion.73
  179.0 2.0 fusion.73
  181.3 2.0 fusion.73
  183.5 2.0 fusion.73
  185.8 2.0 fusion.73
  188.0 2.0 fusion.73
  190.3 2.0 fusion.73
  195.4 101.6 %while.51 = (s32[]{:T(128)}, f32[256,1,8,128]{0,3,2,1:T(8,128)S(1)}, f32[11,2,256,128]{3,2,1,0:T(8,128)}, s32[11]{0:T(128)S(1)}, bf16[11,2,256,128]{3,2,1,0:T(8,...) while((s32[]{:T(128)}, ...), condition=%wide.region_12.13_spmd.clone, body=%wide.region_10.12_spmd.clone.sunk | while | flops 677143552 | bytes 14780849 | solution.py:114
  298.1 1.9 collective-permute-start.10
  300.0 18.9 %collective-permute-done.10 = f32[2,256,128]{2,1,0:T(8,128)S(1)} collective-permute-done((f32[2,256,128]{2,1,0:T(8,128)S(1)}, f32[2,256,128]{2,1,0:T(8,128)S(1)}, u32[]{:S(2)}, u32[]{:S(2)}) %collective-permute-start.10) | collective-permute-done | bytes 262176 | tf_op jit(solution)/shard_map/ppermute | solution.py:17
  321.8 15.8 %collective-permute-done.11 = f32[2,256,128]{2,1,0:T(8,128)S(1)} collective-permute-done((f32[2,256,128]{2,1,0:T(8,128)S(1)}, f32[2,256,128]{2,1,0:T(8,128)S(1)}, u32[]{:S(2)}, u32[]{:S(2)}) %collective-permute-start.11) | collective-permute-done | bytes 262176 | tf_op jit(solution)/shard_map/ppermute | solution.py:17
  340.5 18.1 %collective-permute-done.12 = f32[2,256,128]{2,1,0:T(8,128)S(1)} collective-permute-done((f32[2,256,128]{2,1,0:T(8,128)S(1)}, f32[2,256,128]{2,1,0:T(8,128)S(1)}, u32[]{:S(2)}, u32[]{:S(2)}) %collective-permute-start.12) | collective-permute-done | bytes 262176 | tf_op jit(solution)/shard_map/ppermute | solution.py:17
  361.6 13.9 %collective-permute-done.13 = f32[2,256,128]{2,1,0:T(8,128)S(1)} collective-permute-done((f32[2,256,128]{2,1,0:T(8,128)S(1)}, f32[2,256,128]{2,1,0:T(8,128)S(1)}, u32[]{:S(2)}, u32[]{:S(2)}) %collective-permute-start.13) | collective-permute-done | bytes 262176 | tf_op jit(solution)/shard_map/ppermute | solution.py:17
  375.5 1.9 collective-permute-start.14
  377.5 12.9 %collective-permute-done.14 = f32[2,256,128]{2,1,0:T(8,128)S(1)} collective-permute-done((f32[2,256,128]{2,1,0:T(8,128)S(1)}, f32[2,256,128]{2,1,0:T(8,128)S(1)}, u32[]{:S(2)}, u32[]{:S(2)}) %collective-permute-start.14) | collective-permute-done | bytes 262176 | tf_op jit(solution)/shard_map/ppermute | solution.py:17
  390.4 1.9 collective-permute-start.15
  392.3 13.4 %collective-permute-done.15 = f32[2,256,128]{2,1,0:T(8,128)S(1)} collective-permute-done((f32[2,256,128]{2,1,0:T(8,128)S(1)}, f32[2,256,128]{2,1,0:T(8,128)S(1)}, u32[]{:S(2)}, u32[]{:S(2)}) %collective-permute-start.15) | collective-permute-done | bytes 262176 | tf_op jit(solution)/shard_map/ppermute | solution.py:17
  407.6 14.4 %collective-permute-done.16 = f32[2,256,128]{2,1,0:T(8,128)S(1)} collective-permute-done((f32[2,256,128]{2,1,0:T(8,128)S(1)}, f32[2,256,128]{2,1,0:T(8,128)S(1)}, u32[]{:S(2)}, u32[]{:S(2)}) %collective-permute-start.16) | collective-permute-done | bytes 262176 | tf_op jit(solution)/shard_map/ppermute | solution.py:17
  424.0 14.3 %collective-permute-done.17 = f32[2,256,128]{2,1,0:T(8,128)S(1)} collective-permute-done((f32[2,256,128]{2,1,0:T(8,128)S(1)}, f32[2,256,128]{2,1,0:T(8,128)S(1)}, u32[]{:S(2)}, u32[]{:S(2)}) %collective-permute-start.17) | collective-permute-done | bytes 262176 | tf_op jit(solution)/shard_map/ppermute | solution.py:17
  440.2 14.8 %collective-permute-done.18 = f32[2,256,128]{2,1,0:T(8,128)S(1)} collective-permute-done((f32[2,256,128]{2,1,0:T(8,128)S(1)}, f32[2,256,128]{2,1,0:T(8,128)S(1)}, u32[]{:S(2)}, u32[]{:S(2)}) %collective-permute-start.18) | collective-permute-done | bytes 262176 | tf_op jit(solution)/shard_map/ppermute | solution.py:17
  455.0 1.9 collective-permute-start.19
  459.3 10.3 %collective-permute-done.19 = f32[2,256,128]{2,1,0:T(8,128)S(1)} collective-permute-done((f32[2,256,128]{2,1,0:T(8,128)S(1)}, f32[2,256,128]{2,1,0:T(8,128)S(1)}, u32[]{:S(2)}, u32[]{:S(2)}) %collective-permute-start.19) | collective-permute-done | bytes 262176 | tf_op jit(solution)/shard_map/ppermute | solution.py:17
  (339 shorter events, 135.2 us)
Async XLA Ops:
  0.6 120.2 %copy-start.1 = (bf16[256,1024]{1,0:T(8,128)(2,1)S(1)}, bf16[256,1024]{1,0:T(8,128)(2,1)}, u32[]{:S(2)}) copy-start(bf16[256,1024]{1,0:T(8,128)(2,1)} %param.15) | copy-start | bytes 1572868
  1.6 11.4 %collective-permute-start = (bf16[2,256,128]{2,1,0:T(8,128)(2,1)S(1)}, bf16[2,256,128]{2,1,0:T(8,128)(2,1)S(1)}, u32[]{:S(2)}, u32[]{:S(2)}) collective-permute-start(bf16[2,256,128]{2,1,0:T(8,128)(2,1)S(1)} %pad_maximum_fusion), channel_id=1, source_target_pairs={{0,4},{4,8},{8,12},{12,16},{16,20},{20,24},{24,28},{28,32},{32,36}... | collective-permute-start | bytes 393224 | tf_op jit(solution)/shard_map/ppermute | solution.py:17
  13.0 13.3 %collective-permute-start.1 = (bf16[2,256,128]{2,1,0:T(8,128)(2,1)S(1)}, bf16[2,256,128]{2,1,0:T(8,128)(2,1)S(1)}, u32[]{:S(2)}, u32[]{:S(2)}) collective-permute-start(bf16[2,256,128]{2,1,0:T(8,128)(2,1)S(1)} %collective-permute-done), channel_id=1, source_target_pairs={{0,4},{4,8},{8,12},{12,16},{16,20},{20,24},{24,28},{28,32},{32,36}... | collective-permute-start | bytes 393224 | tf_op jit(solution)/shard_map/ppermute | solution.py:17
  26.3 90.2 %copy-start.5 = (bf16[2,256,128]{2,1,0:T(8,128)(2,1)}, bf16[2,256,128]{2,1,0:T(8,128)(2,1)S(1)}, u32[]{:S(2)}) copy-start(bf16[2,256,128]{2,1,0:T(8,128)(2,1)S(1)} %collective-permute-done.1) | copy-start | bytes 393220
  26.3 13.3 %collective-permute-start.2 = (bf16[2,256,128]{2,1,0:T(8,128)(2,1)S(1)}, bf16[2,256,128]{2,1,0:T(8,128)(2,1)S(1)}, u32[]{:S(2)}, u32[]{:S(2)}) collective-permute-start(bf16[2,256,128]{2,1,0:T(8,128)(2,1)S(1)} %collective-permute-done.1), channel_id=1, source_target_pairs={{0,4},{4,8},{8,12},{12,16},{16,20},{20,24},{24,28},{28,32},{32,36}... | collective-permute-start | bytes 393224 | tf_op jit(solution)/shard_map/ppermute | solution.py:17
  39.6 77.0 %copy-start.7 = (bf16[2,256,128]{2,1,0:T(8,128)(2,1)}, bf16[2,256,128]{2,1,0:T(8,128)(2,1)S(1)}, u32[]{:S(2)}) copy-start(bf16[2,256,128]{2,1,0:T(8,128)(2,1)S(1)} %collective-permute-done.2) | copy-start | bytes 393220
  39.6 13.3 %collective-permute-start.3 = (bf16[2,256,128]{2,1,0:T(8,128)(2,1)S(1)}, bf16[2,256,128]{2,1,0:T(8,128)(2,1)S(1)}, u32[]{:S(2)}, u32[]{:S(2)}) collective-permute-start(bf16[2,256,128]{2,1,0:T(8,128)(2,1)S(1)} %collective-permute-done.2), channel_id=1, source_target_pairs={{0,4},{4,8},{8,12},{12,16},{16,20},{20,24},{24,28},{28,32},{32,36}... | collective-permute-start | bytes 393224 | tf_op jit(solution)/shard_map/ppermute | solution.py:17
  52.9 63.7 %copy-start.8 = (bf16[2,256,128]{2,1,0:T(8,128)(2,1)}, bf16[2,256,128]{2,1,0:T(8,128)(2,1)S(1)}, u32[]{:S(2)}) copy-start(bf16[2,256,128]{2,1,0:T(8,128)(2,1)S(1)} %collective-permute-done.3) | copy-start | bytes 393220
  52.9 13.2 %collective-permute-start.4 = (bf16[2,256,128]{2,1,0:T(8,128)(2,1)S(1)}, bf16[2,256,128]{2,1,0:T(8,128)(2,1)S(1)}, u32[]{:S(2)}, u32[]{:S(2)}) collective-permute-start(bf16[2,256,128]{2,1,0:T(8,128)(2,1)S(1)} %collective-permute-done.3), channel_id=1, source_target_pairs={{0,4},{4,8},{8,12},{12,16},{16,20},{20,24},{24,28},{28,32},{32,36}... | collective-permute-start | bytes 393224 | tf_op jit(solution)/shard_map/ppermute | solution.py:17
  66.0 50.6 %copy-start.9 = (bf16[2,256,128]{2,1,0:T(8,128)(2,1)}, bf16[2,256,128]{2,1,0:T(8,128)(2,1)S(1)}, u32[]{:S(2)}) copy-start(bf16[2,256,128]{2,1,0:T(8,128)(2,1)S(1)} %collective-permute-done.4) | copy-start | bytes 393220
  66.0 13.2 %collective-permute-start.5 = (bf16[2,256,128]{2,1,0:T(8,128)(2,1)S(1)}, bf16[2,256,128]{2,1,0:T(8,128)(2,1)S(1)}, u32[]{:S(2)}, u32[]{:S(2)}) collective-permute-start(bf16[2,256,128]{2,1,0:T(8,128)(2,1)S(1)} %collective-permute-done.4), channel_id=1, source_target_pairs={{0,4},{4,8},{8,12},{12,16},{16,20},{20,24},{24,28},{28,32},{32,36}... | collective-permute-start | bytes 393224 | tf_op jit(solution)/shard_map/ppermute | solution.py:17
  79.2 37.4 %copy-start.10 = (bf16[2,256,128]{2,1,0:T(8,128)(2,1)}, bf16[2,256,128]{2,1,0:T(8,128)(2,1)S(1)}, u32[]{:S(2)}) copy-start(bf16[2,256,128]{2,1,0:T(8,128)(2,1)S(1)} %collective-permute-done.5) | copy-start | bytes 393220
  79.2 13.3 %collective-permute-start.6 = (bf16[2,256,128]{2,1,0:T(8,128)(2,1)S(1)}, bf16[2,256,128]{2,1,0:T(8,128)(2,1)S(1)}, u32[]{:S(2)}, u32[]{:S(2)}) collective-permute-start(bf16[2,256,128]{2,1,0:T(8,128)(2,1)S(1)} %collective-permute-done.5), channel_id=1, source_target_pairs={{0,4},{4,8},{8,12},{12,16},{16,20},{20,24},{24,28},{28,32},{32,36}... | collective-permute-start | bytes 393224 | tf_op jit(solution)/shard_map/ppermute | solution.py:17
  92.5 27.1 %copy-start.11 = (bf16[2,256,128]{2,1,0:T(8,128)(2,1)}, bf16[2,256,128]{2,1,0:T(8,128)(2,1)S(1)}, u32[]{:S(2)}) copy-start(bf16[2,256,128]{2,1,0:T(8,128)(2,1)S(1)} %collective-permute-done.6) | copy-start | bytes 393220
  92.5 13.2 %collective-permute-start.7 = (bf16[2,256,128]{2,1,0:T(8,128)(2,1)S(1)}, bf16[2,256,128]{2,1,0:T(8,128)(2,1)}, u32[]{:S(2)}, u32[]{:S(2)}) collective-permute-start(bf16[2,256,128]{2,1,0:T(8,128)(2,1)S(1)} %collective-permute-done.6), channel_id=1, source_target_pairs={{0,4},{4,8},{8,12},{12,16},{16,20},{20,24},{24,28},{28,32},{32,36}... | collective-permute-start | bytes 393224 | tf_op jit(solution)/shard_map/ppermute | solution.py:17
  105.7 18.5 %collective-permute-start.8 = (bf16[2,256,128]{2,1,0:T(8,128)(2,1)}, bf16[2,256,128]{2,1,0:T(8,128)(2,1)}, u32[]{:S(2)}, u32[]{:S(2)}) collective-permute-start(bf16[2,256,128]{2,1,0:T(8,128)(2,1)} %collective-permute-done.7), channel_id=1, source_target_pairs={{0,4},{4,8},{8,12},{12,16},{16,20},{20,24},{24,28},{28,32},{32,36}... | collective-permute-start | bytes 393224 | tf_op jit(solution)/shard_map/ppermute | solution.py:17
  122.8 19.8 %copy-start.3 = (bf16[256,128]{1,0:T(8,128)(2,1)S(1)}, bf16[256,128]{1,0:T(8,128)(2,1)}, u32[]{:S(2)}) copy-start(bf16[256,128]{1,0:T(8,128)(2,1)} %param.13) | copy-start | bytes 196612
  122.8 19.9 %copy-start.4 = (bf16[256,128]{1,0:T(8,128)(2,1)S(1)}, bf16[256,128]{1,0:T(8,128)(2,1)}, u32[]{:S(2)}) copy-start(bf16[256,128]{1,0:T(8,128)(2,1)} %param.12) | copy-start | bytes 196612
  124.1 18.4 %copy-start.6 = (bf16[2,256,128]{2,1,0:T(8,128)(2,1)S(1)}, bf16[2,256,128]{2,1,0:T(8,128)(2,1)}, u32[]{:S(2)}) copy-start(bf16[2,256,128]{2,1,0:T(8,128)(2,1)} %copy-done.5) | copy-start | bytes 393220
  124.2 11.8 %collective-permute-start.9 = (bf16[2,256,128]{2,1,0:T(8,128)(2,1)}, bf16[2,256,128]{2,1,0:T(8,128)(2,1)S(1)}, u32[]{:S(2)}, u32[]{:S(2)}) collective-permute-start(bf16[2,256,128]{2,1,0:T(8,128)(2,1)} %collective-permute-done.8), channel_id=1, source_target_pairs={{0,4},{4,8},{8,12},{12,16},{16,20},{20,24},{24,28},{28,32},{32,36}... | collective-permute-start | bytes 393224 | tf_op jit(solution)/shard_map/ppermute | solution.py:17
  142.7 1.1 copy-start.2
  297.0 78.5 %copy-start = (f32[11,2,256,128]{3,2,1,0:T(8,128)S(1)}, f32[11,2,256,128]{3,2,1,0:T(8,128)}, u32[]{:S(2)}) copy-start(f32[11,2,256,128]{3,2,1,0:T(8,128)} %get-tuple-element.677) | copy-start | bytes 8650756
  298.1 20.8 %collective-permute-start.10 = (f32[2,256,128]{2,1,0:T(8,128)S(1)}, f32[2,256,128]{2,1,0:T(8,128)S(1)}, u32[]{:S(2)}, u32[]{:S(2)}) collective-permute-start(f32[2,256,128]{2,1,0:T(8,128)S(1)} %slice_bitcast_fusion), channel_id=1, source_target_pairs={{4,0},{8,4},{12,8},{16,12},{20,16},{24,20},{28,24},{32,28},{36,32}... | collective-permute-start | bytes 786440 | tf_op jit(solution)/shard_map/ppermute | solution.py:17
  319.9 17.7 %collective-permute-start.11 = (f32[2,256,128]{2,1,0:T(8,128)S(1)}, f32[2,256,128]{2,1,0:T(8,128)S(1)}, u32[]{:S(2)}, u32[]{:S(2)}) collective-permute-start(f32[2,256,128]{2,1,0:T(8,128)S(1)} %bitcast_add_fusion.10), channel_id=1, source_target_pairs={{4,0},{8,4},{12,8},{16,12},{20,16},{24,20},{28,24},{32,28},{36,32}... | collective-permute-start | bytes 786440 | tf_op jit(solution)/shard_map/ppermute | solution.py:17
  338.6 20.1 %collective-permute-start.12 = (f32[2,256,128]{2,1,0:T(8,128)S(1)}, f32[2,256,128]{2,1,0:T(8,128)S(1)}, u32[]{:S(2)}, u32[]{:S(2)}) collective-permute-start(f32[2,256,128]{2,1,0:T(8,128)S(1)} %bitcast_add_fusion.9), channel_id=1, source_target_pairs={{4,0},{8,4},{12,8},{16,12},{20,16},{24,20},{28,24},{32,28},{36,32}... | collective-permute-start | bytes 786440 | tf_op jit(solution)/shard_map/ppermute | solution.py:17
  359.6 15.9 %collective-permute-start.13 = (f32[2,256,128]{2,1,0:T(8,128)S(1)}, f32[2,256,128]{2,1,0:T(8,128)S(1)}, u32[]{:S(2)}, u32[]{:S(2)}) collective-permute-start(f32[2,256,128]{2,1,0:T(8,128)S(1)} %bitcast_add_fusion.8), channel_id=1, source_target_pairs={{4,0},{8,4},{12,8},{16,12},{20,16},{24,20},{28,24},{32,28},{36,32}... | collective-permute-start | bytes 786440 | tf_op jit(solution)/shard_map/ppermute | solution.py:17
  375.5 14.8 %collective-permute-start.14 = (f32[2,256,128]{2,1,0:T(8,128)S(1)}, f32[2,256,128]{2,1,0:T(8,128)S(1)}, u32[]{:S(2)}, u32[]{:S(2)}) collective-permute-start(f32[2,256,128]{2,1,0:T(8,128)S(1)} %bitcast_add_fusion.7), channel_id=1, source_target_pairs={{4,0},{8,4},{12,8},{16,12},{20,16},{24,20},{28,24},{32,28},{36,32}... | collective-permute-start | bytes 786440 | tf_op jit(solution)/shard_map/ppermute | solution.py:17
  390.4 15.3 %collective-permute-start.15 = (f32[2,256,128]{2,1,0:T(8,128)S(1)}, f32[2,256,128]{2,1,0:T(8,128)S(1)}, u32[]{:S(2)}, u32[]{:S(2)}) collective-permute-start(f32[2,256,128]{2,1,0:T(8,128)S(1)} %bitcast_add_fusion.6), channel_id=1, source_target_pairs={{4,0},{8,4},{12,8},{16,12},{20,16},{24,20},{28,24},{32,28},{36,32}... | collective-permute-start | bytes 786440 | tf_op jit(solution)/shard_map/ppermute | solution.py:17
  405.7 16.4 %collective-permute-start.16 = (f32[2,256,128]{2,1,0:T(8,128)S(1)}, f32[2,256,128]{2,1,0:T(8,128)S(1)}, u32[]{:S(2)}, u32[]{:S(2)}) collective-permute-start(f32[2,256,128]{2,1,0:T(8,128)S(1)} %bitcast_add_fusion.5), channel_id=1, source_target_pairs={{4,0},{8,4},{12,8},{16,12},{20,16},{24,20},{28,24},{32,28},{36,32}... | collective-permute-start | bytes 786440 | tf_op jit(solution)/shard_map/ppermute | solution.py:17
  422.1 16.2 %collective-permute-start.17 = (f32[2,256,128]{2,1,0:T(8,128)S(1)}, f32[2,256,128]{2,1,0:T(8,128)S(1)}, u32[]{:S(2)}, u32[]{:S(2)}) collective-permute-start(f32[2,256,128]{2,1,0:T(8,128)S(1)} %bitcast_add_fusion.4), channel_id=1, source_target_pairs={{4,0},{8,4},{12,8},{16,12},{20,16},{24,20},{28,24},{32,28},{36,32}... | collective-permute-start | bytes 786440 | tf_op jit(solution)/shard_map/ppermute | solution.py:17
  438.3 16.7 %collective-permute-start.18 = (f32[2,256,128]{2,1,0:T(8,128)S(1)}, f32[2,256,128]{2,1,0:T(8,128)S(1)}, u32[]{:S(2)}, u32[]{:S(2)}) collective-permute-start(f32[2,256,128]{2,1,0:T(8,128)S(1)} %bitcast_add_fusion.3), channel_id=1, source_target_pairs={{4,0},{8,4},{12,8},{16,12},{20,16},{24,20},{28,24},{32,28},{36,32}... | collective-permute-start | bytes 786440 | tf_op jit(solution)/shard_map/ppermute | solution.py:17
  455.0 14.6 %collective-permute-start.19 = (f32[2,256,128]{2,1,0:T(8,128)S(1)}, f32[2,256,128]{2,1,0:T(8,128)S(1)}, u32[]{:S(2)}, u32[]{:S(2)}) collective-permute-start(f32[2,256,128]{2,1,0:T(8,128)S(1)} %bitcast_add_fusion.2), channel_id=1, source_target_pairs={{4,0},{8,4},{12,8},{16,12},{20,16},{24,20},{28,24},{32,28},{36,32}... | collective-permute-start | bytes 786440 | tf_op jit(solution)/shard_map/ppermute | solution.py:17
where the time goes:
time: 475 us; the launch traced here: 471 us
  waiting for transfers between devices  173 us (36%)
  starting transfers between devices  120 us (25%)
  matrix products  91.4 us (19%)
  loops' own time  30.4 us (6%)
  other arithmetic  29.7 us (6%)
  local copies, waits for them, and re-layouts  26.2 us (6%)
    ppermute x20, waiting for transfers between devices, from_behind(): return lax.ppermute(block, axis, route)  173 us
    ppermute x20, starting transfers between devices, from_behind(): return lax.ppermute(block, axis, route)  120 us
    dot_general x22, matrix products, scored(): jnp.einsum('tkgd,skd->kgts', q_heads, current_key, preferred_element_type...  31.7 us
    another operation x1, loops' own time, body(): lax.scan(third_pass, jnp.zeros(head_shape, jnp.float32), jnp.arange(reach...  29.1 us
    dot_general x11, matrix products, second_pass(): jnp.einsum('kgts,skd->tkgd', probabilities_reduced, current_value, prefer...  21.6 us
    unnamed x40, local copies, waits for them, and re-layouts  15.6 us
    dot_general x11, matrix products, third_pass(): jnp.einsum('kgts,skd->tkgd', score_gradient, current_key, preferred_eleme...  14.4 us
    dot_general x11, matrix products, third_pass(): jnp.einsum('tkgd,skd->kgts', g_heads, current_value, preferred_element_ty...  14.2 us
  transfers between devices with their start and end apart: 20, of which 19 were waited for; matrix products, arithmetic and copies ran while one was open for 2% of the time, Pallas kernels for 0%

commit v1 on v0

v1 whole, which is shorter than its diff:
```python
import jax
import jax.numpy as jnp
from jax import lax
from jax.experimental import pallas as pl
from jax.experimental.pallas import tpu as pltpu
from jax.sharding import PartitionSpec as P

HEADS = 8
TOK = 256
DIM = 128
BLOCKS = 11
SLOTS = 15
FACTOR = DIM ** -0.5
EXP2 = FACTOR * 1.4426950408889634
NEG = -1e30
MESH = pl.DeviceIdType.MESH
F32, BF16 = jnp.float32, jnp.bfloat16

FETCH = ((0, 0), (1, 0), (0, 1), (0, 3), (2, 0), (1, 1), (1, 3), (0, 2), (2, 1), (2, 3), (1, 2), (3, 1), (3, 2), (2, 2))
RETURN = ((3, 1), (3, 2), (2, 2), (2, 1), (2, 3), (2, 0), (1, 2), (1, 1), (1, 3), (1, 0), (0, 2), (0, 1), (0, 3), (0, 0))


def dot_nt(a, b):
    return lax.dot_general(a, b, (((1,), (1,)), ((), ())), preferred_element_type=F32)


def dot_nn(a, b):
    return lax.dot_general(a, b, (((1,), (0,)), ((), ())), preferred_element_type=F32)


def pick(table, column, step):
    value = jnp.int32(0)
    for at, entry in enumerate(table):
        if entry[column]:
            value = value + entry[column] * (step == at).astype(jnp.int32)
    return value


def kernel(q, k, v, lengths, g, out, dq, dk, dv,
           kb, vb, s_sc, d_sc, m_sc, dl_sc, acc_q, qt, gt, th, bias,
           gk, gv, mid, side, row, tri,
           f_send, f_recv, c_send, c_recv, o_send, mid_recv, side_recv, row_recv, tri_send, tri_recv, far_send):
    me = lax.axis_index("ctx")
    size = lax.axis_size("ctx")
    x = me % 4
    y = (me // 4) % 4
    plane = me // 16
    base = me - x
    right, left = base + (x + 1) % 4, base + (x + 3) % 4

    def at_row(planes, r, c):
        return ((me // 16 + planes + size // 16) % (size // 16)) * 16 + r * 4 + c

    def slot(kk, j, col):
        return (4 * kk + j - 4 * ((col + j) // 4) + SLOTS) % SLOTS

    def remote(src, dst, send, recv, ctx):
        return pltpu.make_async_remote_copy(src_ref=src, dst_ref=dst, send_sem=send, recv_sem=recv,
                                            device_id={"ctx": ctx}, device_id_type=MESH)


    def far_pairs(act):
        for r in (1, 2, 3):
            for c in (0, 1):
                act((y == 0) & (x >= 2 + c), at_row(0, r, c), r, c)
        for c in (0, 1):
            act((y == 1) & (x >= 2 + c), at_row(1, 0, c), 0, c)

    barrier = pltpu.get_barrier_semaphore()

    def greet(ctx):
        pl.semaphore_signal(barrier, inc=1, device_id={"ctx": ctx}, device_id_type=MESH)

    for ctx in (right, left, (me + 4) % size, (me + size - 4) % size, (me + 8) % size, (me + size - 8) % size):
        greet(ctx)
    far_pairs(lambda on, ctx, r, c: pl.when(on)(lambda: greet(ctx)))
    for c in (0, 1):
        for s in (2 + c, 3) if c == 0 else (3,):
            @pl.when((x == c) & (y > 0))
            def _():
                greet(at_row(0, 0, s))

            @pl.when((x == c) & (y == 0))
            def _():
                greet(at_row(-1, 1, s))
    given = jnp.where(x >= 2, x - 1, 0) * jnp.where(y == 0, 3, jnp.where(y == 1, 1, 0))
    taken = jnp.where(x <= 1, 2 - x, 0)
    pl.semaphore_wait(barrier, 6 + given + taken)

    def column_copies(kk):
        ctx = (me + 4 * kk) % size
        return [remote(src, buf.at[4 * kk], c_send.at[n, kk], f_recv.at[n, 4 * kk], ctx)
                for n, (src, buf) in enumerate(((k, kb), (v, vb)))]

    def row_copies(kk):
        copies = []
        for n, buf in enumerate((kb, vb)):
            for side_no, (j, ctx) in enumerate(((1, right), (3, left))):
                to = slot(kk, j, x)
                copies.append(remote(buf.at[4 * kk], buf.at[to], f_send.at[n, kk, side_no], f_recv.at[n, to], ctx))
        return copies

    def onward_key(kk):
        col = (x + 3) % 4
        to = slot(kk, 2, col)
        return remote(kb.at[slot(kk, 1, col)], kb.at[to], f_send.at[0, kk, 2], f_recv.at[0, to], right)

    def onward_value(kk):
        col = (x + 1) % 4
        to = slot(kk, 2, col)
        return remote(vb.at[slot(kk, 3, col)], vb.at[to], f_send.at[1, kk, 2], f_recv.at[1, to], left)

    def far_copies(r, c, ctx):
        src = (4 * (3 - r)) if r else 0
        to = 12 + (c - x)
        return [remote(buf.at[src], buf.at[to], far_send.at[n, (r + 3) % 4 if r else 2, c], f_recv.at[n, to], ctx)
                for n, buf in enumerate((kb, vb))]

    def start_far(rows):
        def act(on, ctx, r, c):
            if r in rows:
                @pl.when(on)
                def _():
                    for copy in far_copies(r, c, ctx):
                        copy.start()
        far_pairs(act)

    for kk in (1, 2):
        for copy in column_copies(kk):
            copy.start()
    kb[0] = k[...]
    vb[0] = v[...]
    for copy in row_copies(0):
        copy.start()
    start_far((3, 0))

    start = jnp.full((TOK, DIM), -1, jnp.int32) * (me * TOK)
    token = lax.broadcasted_iota(jnp.int32, (TOK, DIM), 0)
    end = -me * TOK
    for doc in range(lengths.shape[0]):
        end = end + lengths[doc]
        start = jnp.where(token >= end, end, start)
    th[...] = start
    for h in range(HEADS):
        cols = slice(h * DIM, (h + 1) * DIM)
        qt[h] = q[:, cols].T
        gt[h] = g[:, cols].T
    m_sc[...] = jnp.full_like(m_sc, NEG)

    def arrived(at):
        for n, buf in enumerate((kb, vb)):
            remote(buf.at[at], buf.at[at], f_send.at[0, 0, 0], f_recv.at[n, at], right).wait_recv()

    def scores(d):
        key_at = lax.broadcasted_iota(jnp.int32, (TOK, DIM), 1) - d * TOK
        query_at = lax.broadcasted_iota(jnp.int32, (TOK, DIM), 0)
        for part in (0, 1):
            at = key_at + part * DIM
            seen = (at >= th[...]) & (at <= query_at)
            bias[:, part * DIM:(part + 1) * DIM] = jnp.where(seen, 0.0, NEG)
        key, value = kb[d], vb[d]
        for h in range(HEADS):
            cols = slice(h * DIM, (h + 1) * DIM)
            s = dot_nt(q[:, cols], key) + bias[...]
            s_sc[h, d] = s
            m_sc[h] = jnp.maximum(m_sc[h], jnp.maximum(s[:, :DIM], s[:, DIM:]))
            d_sc[h, d] = dot_nt(g[:, cols], value)

    def valid(kk, j):
        wraps = (j > x).astype(jnp.int32)
        d = 4 * kk + j - 4 * wraps
        return (d >= 0) & (d < BLOCKS), d

    def fetch_step(step, _):
        kk, j = pick(FETCH, 0, step), pick(FETCH, 1, step)
        ok, d = valid(kk, j)
        there = (d + SLOTS) % SLOTS

        @pl.when((step > 0) & (ok | (kk < 3)))
        def _():
            arrived(there)

        @pl.when((j == 0) & (kk > 0))
        def _():
            for copy in row_copies(kk):
                copy.start()

        @pl.when((j == 0) & (kk == 1))
        def _():
            start_far((2,))

        @pl.when((j == 0) & (kk == 2))
        def _():
            start_far((1,))

        @pl.when((j == 1) & (kk < 3))
        def _():
            onward_key(kk).start()

        @pl.when((j == 3) & (kk < 3))
        def _():
            onward_value(kk).start()

        @pl.when(ok)
        def _():
            scores(there)

        return 0

    lax.fori_loop(0, len(FETCH), fetch_step, 0)

    def finish_head(h, _):
        m = jnp.max(m_sc[h], axis=1, keepdims=True)
        total = jnp.zeros((TOK, 2 * DIM), F32)
        ones = jnp.ones((TOK, DIM), BF16)
        for d in range(BLOCKS):
            p = jnp.exp2((s_sc[h, d] - m) * EXP2).astype(BF16)
            total = total + dot_nn(p, jnp.concatenate([vb[d], ones], 1))
        norm = total[:, DIM:]
        full = total[:, :DIM] / norm
        acc_q[h] = full
        m_sc[h] = m * EXP2 + jnp.log2(norm)
        return 0

    lax.fori_loop(0, HEADS, finish_head, 0)
    for h in range(HEADS):
        cols = slice(h * DIM, (h + 1) * DIM)
        full = acc_q[h]
        out[:, cols] = full.astype(BF16)
        delta = jnp.sum(full * g[:, cols].astype(F32), axis=1, keepdims=True)
        dl_sc[h] = jnp.broadcast_to(delta, (TOK, DIM))
    acc_q[...] = jnp.zeros_like(acc_q)

    def gradients(d):
        key = kb[d]
        key_part = value_part = None
        for h in range(HEADS):
            lse, delta = m_sc[h], dl_sc[h]
            p = jnp.exp2(s_sc[h, d] * EXP2 - jnp.concatenate([lse, lse], 1))
            ds = (p * (d_sc[h, d] - jnp.concatenate([delta, delta], 1))).astype(BF16)
            acc_q[h] += dot_nn(ds, key)
            a, b = dot_nn(qt[h], ds), dot_nn(gt[h], p.astype(BF16))
            key_part = a if h == 0 else key_part + a
            value_part = b if h == 0 else value_part + b
        gk[d] = key_part.astype(BF16)
        gv[d] = value_part.astype(BF16)

    def add(ref, at, *others):
        total = ref[at].astype(F32)
        for other in others:
            total = total + other.astype(F32)
        ref[at] = total.astype(BF16)

    def mid_copy(n, kk, at):
        buf, ctx = ((gk, left), (gv, right))[n]
        return remote(buf.at[at], mid.at[n, kk], o_send.at[n, kk, 2], mid_recv.at[n, kk], ctx)

    def side_copies(kk, at, side_no, ctx):
        return [remote(buf.at[at], side.at[n, kk, side_no], o_send.at[n, kk, side_no], side_recv.at[n, kk, side_no], ctx)
                for n, buf in enumerate((gk, gv))]

    def home_copies(kk):
        ctx = (me + size - 4 * kk) % size
        return [remote(buf.at[4 * kk], row.at[n, kk], c_send.at[n, kk], row_recv.at[n, kk], ctx)
                for n, buf in enumerate((gk, gv))]

    def tri_copies(d):
        col = 12 + x - d
        where = jnp.where(y == 0, at_row(-1, 1, col), at_row(0, 0, col))
        index = jnp.where(y == 0, 2, y - 1)
        return [remote(buf.at[d], tri.at[n, index, x], tri_send.at[n, d - 9], tri_recv.at[n, index, x], where)
                for n, buf in enumerate((gk, gv))]

    def take_tri(kk):
        index = 2 - kk
        for c in (0, 1):
            @pl.when((x >= 2 + c) & ((y == 0) | ((y == 1) & (kk == 0))))
            def _():
                for n, buf in enumerate((gk, gv)):
                    remote(tri.at[n, index, c], tri.at[n, index, c], tri_send.at[n, 0], tri_recv.at[n, index, c],
                           right).wait_recv()
                    add(buf, 4 * kk, tri[n, index, c])

    def return_step(step, _):
        kk, j = pick(RETURN, 0, step), pick(RETURN, 1, step)
        ok, d = valid(kk, j)
        there = (d + SLOTS) % SLOTS

        @pl.when(ok)
        def _():
            gradients(there)

        @pl.when(jnp.logical_not(ok) & (kk < 3))
        def _():
            gk[there] = jnp.zeros((DIM, TOK), BF16)
            gv[there] = jnp.zeros((DIM, TOK), BF16)

        @pl.when((kk == 3) & ok)
        def _():
            for copy in tri_copies(there):
                copy.start()

        @pl.when((j == 2) & (kk < 3))
        def _():
            mid_copy(0, kk, there).start()
            mid_copy(1, kk, there).start()

        @pl.when((j == 1) & (kk < 3))
        def _():
            mid_copy(0, kk, there).wait_recv()
            add(gk, there, mid[0, kk])
            for copy in side_copies(kk, there, 0, left):
                copy.start()

        @pl.when((j == 3) & (kk < 3))
        def _():
            mid_copy(1, kk, there).wait_recv()
            add(gv, there, mid[1, kk])
            for copy in side_copies(kk, there, 1, right):
                copy.start()

        @pl.when(j == 0)
        def _():
            for side_no in (0, 1):
                for copy in side_copies(kk, there, side_no, right):
                    copy.wait_recv()
            for n, buf in enumerate((gk, gv)):
                add(buf, there, side[n, kk, 0], side[n, kk, 1])
            take_tri(kk)

            @pl.when(kk > 0)
            def _():
                for copy in home_copies(kk):
                    copy.start()

        return 0

    for kk in (1, 2):
        for copy in column_copies(kk):
            copy.wait_send()
    lax.fori_loop(0, len(RETURN), return_step, 0)

    for h in range(HEADS):
        dq[:, h * DIM:(h + 1) * DIM] = (acc_q[h] * FACTOR).astype(BF16)
    for kk in (1, 2):
        for copy in home_copies(kk):
            copy.wait_recv()
    for n, (buf, to) in enumerate(((gk, dk), (gv, dv))):
        total = buf[0].astype(F32) + row[n, 1].astype(F32) + row[n, 2].astype(F32)
        to[...] = (total * FACTOR if n == 0 else total).T

    def end_sends(kk, _):
        for copy in row_copies(kk):
            copy.wait_send()
        onward_key(kk).wait_send()
        onward_value(kk).wait_send()
        mid_copy(0, kk, 0).wait_send()
        mid_copy(1, kk, 0).wait_send()
        for side_no in (0, 1):
            for copy in side_copies(kk, 0, side_no, right):
                copy.wait_send()
        return 0

    lax.fori_loop(0, 3, end_sends, 0)
    for kk in (1, 2):
        for copy in home_copies(kk):
            copy.wait_send()

    def end_far(on, ctx, r, c):
        @pl.when(on)
        def _():
            for copy in far_copies(r, c, ctx):
                copy.wait_send()
    far_pairs(end_far)
    for d in (9, 10):
        @pl.when(x <= d - 9)
        def _():
            for copy in tri_copies(d):
                copy.wait_send()


def body(queries, keys, values, lengths, output_gradient):
    vmem = pl.BlockSpec(memory_space=pltpu.VMEM)
    wide = (TOK, HEADS * DIM)
    dma = pltpu.SemaphoreType.DMA
    out, dq, dk, dv = pl.pallas_call(
        kernel,
        out_shape=[
            jax.ShapeDtypeStruct(wide, BF16),
            jax.ShapeDtypeStruct(wide, BF16),
            jax.ShapeDtypeStruct((TOK, DIM), F32),
            jax.ShapeDtypeStruct((TOK, DIM), F32),
        ],
        in_specs=[vmem, vmem, vmem, pl.BlockSpec(memory_space=pltpu.SMEM), vmem],
        out_specs=[vmem] * 4,
        scratch_shapes=[
            pltpu.VMEM((SLOTS, TOK, DIM), BF16),
            pltpu.VMEM((SLOTS, TOK, DIM), BF16),
            pltpu.VMEM((HEADS, BLOCKS, TOK, TOK), F32),
            pltpu.VMEM((HEADS, BLOCKS, TOK, TOK), F32),
            pltpu.VMEM((HEADS, TOK, DIM), F32),
            pltpu.VMEM((HEADS, TOK, DIM), F32),
            pltpu.VMEM((HEADS, TOK, DIM), F32),
            pltpu.VMEM((HEADS, DIM, TOK), BF16),
            pltpu.VMEM((HEADS, DIM, TOK), BF16),
            pltpu.VMEM((TOK, DIM), jnp.int32),
            pltpu.VMEM((TOK, TOK), F32),
            pltpu.VMEM((SLOTS, DIM, TOK), BF16),
            pltpu.VMEM((SLOTS, DIM, TOK), BF16),
            pltpu.VMEM((2, 3, DIM, TOK), BF16),
            pltpu.VMEM((2, 3, 2, DIM, TOK), BF16),
            pltpu.VMEM((2, 3, DIM, TOK), BF16),
            pltpu.VMEM((2, 3, 2, DIM, TOK), BF16),
            dma((2, 3, 3)),
            dma((2, SLOTS)),
            dma((2, 3)),
            dma((2, 3)),
            dma((2, 3, 3)),
            dma((2, 3)),
            dma((2, 3, 2)),
            dma((2, 3)),
            dma((2, 2)),
            dma((2, 3, 2)),
            dma((2, 4, 2)),
        ],
        compiler_params=pltpu.CompilerParams(
            collective_id=0, has_side_effects=True, vmem_limit_bytes=62 << 20
        ),
    )(queries, keys, values, lengths, output_gradient)
    return out, dq.astype(F32), dk, dv


def solution(mesh):
    spec = P("ctx", "head")
    return jax.shard_map(
        body,
        mesh=mesh,
        in_specs=(spec, spec, spec, P(), spec),
        out_specs=(spec, spec, spec, spec),
        check_vma=False,
    )
```

time: 475 us -> 91 us (0.19)
  the two profiles are of different devices: /device:TPU:94 before, /device:TPU:32 now
where the time goes in v1:
time: 91 us; the launch traced here: 90.8 us
  Pallas kernels  85.3 us (94%)
  local copies, waits for them, and re-layouts  2.63 us (3%)
  other arithmetic  2.18 us (2%)
    pallas_call x1, Pallas kernels, body(): pl.pallas_call(kernel, out_shape=[jax.ShapeDtypeStruct(wide, BF16), jax.S...  85.3 us
    unnamed x9, local copies, waits for them, and re-layouts  2.63 us
    convert_element_type x1, other arithmetic, body(): return (out, dq.astype(F32), dk, dv)  2.18 us

profile of v1, /device:TPU:32, one launch (start us, length us, event | category | flops | bytes accessed | tf_op | source)
XLA Modules:
  0.0 90.8 jit_solution(11239074631095301193)
XLA Ops:
  0.6 85.3 %shard_map.84 = (bf16[256,1024]{1,0:T(8,128)(2,1)}, bf16[256,1024]{1,0:T(8,128)(2,1)}, f32[256,128]{1,0:T(8,128)}, f32[256,128]{1,0:T(8,128)}) custom-call(bf16[256,1024]{1,0:T(8,128)(2,1)} %q.1, bf16[256,128]{1,0:T(8,128)(2,1)} %k.1, bf16[256,128]{1,0:T(8,128)(2,1)} %v.1, s32[32]{0:T(128)} %lengths.1, bf16[256,1024]{1,0:T(8,128)(2,1)} %g.1), custom_call_target="tpu_custom_call" | custom-call | tf_op jit(solution)/shard_map/pallas_call | solution.py:386
  86.0 0.0 copy-start
  86.0 2.2 %convert_element_type.3 = f32[256,1024]{1,0:T(8,128)} convert(bf16[256,1024]{1,0:T(8,128)(2,1)} %get-tuple-element.9) | non-fusion elementwise | flops 262144 | bytes 1572864 | tf_op jit(solution)/shard_map/convert_element_type | solution.py:430
  88.2 0.0 copy-done
  88.2 0.0 copy-start.2
  88.2 0.8 copy.12
  89.0 0.2 copy-done.2
  89.2 0.0 copy-start.1
  89.2 0.7 copy.13
  89.9 0.3 copy-done.1
  90.2 0.7 copy.14
Async XLA Ops:
  86.0 2.2 %copy-start = (bf16[256,1024]{1,0:T(8,128)(2,1)S(1)}, bf16[256,1024]{1,0:T(8,128)(2,1)}, u32[]{:S(2)}) copy-start(bf16[256,1024]{1,0:T(8,128)(2,1)} %get-tuple-element.16) | copy-start | bytes 1572868
  88.2 1.0 %copy-start.2 = (f32[256,128]{1,0:T(8,128)S(1)}, f32[256,128]{1,0:T(8,128)}, u32[]{:S(2)}) copy-start(f32[256,128]{1,0:T(8,128)} %get-tuple-element.18) | copy-start | bytes 393220
  89.2 1.0 %copy-start.1 = (f32[256,128]{1,0:T(8,128)S(1)}, f32[256,128]{1,0:T(8,128)}, u32[]{:S(2)}) copy-start(f32[256,128]{1,0:T(8,128)} %get-tuple-element.19) | copy-start | bytes 393220

commit v2 on v1

v2 whole, which is shorter than its diff:
```python
import jax
import jax.numpy as jnp
from jax import lax
from jax.experimental import pallas as pl
from jax.experimental.pallas import tpu as pltpu
from jax.sharding import PartitionSpec as P

HEADS = 8
TOK = 256
DIM = 128
BLOCKS = 11
SLOTS = 15
FACTOR = DIM ** -0.5
EXP2 = FACTOR * 1.4426950408889634
NEG = -1e30
MESH = pl.DeviceIdType.MESH
F32, BF16 = jnp.float32, jnp.bfloat16


def dot_nt(a, b):
    return lax.dot_general(a, b, (((1,), (1,)), ((), ())), preferred_element_type=F32)


def dot_nn(a, b):
    return lax.dot_general(a, b, (((1,), (0,)), ((), ())), preferred_element_type=F32)


def pick(table, column, step):
    value = jnp.int32(0)
    for at, entry in enumerate(table):
        if entry[column]:
            value = value + entry[column] * (step == at).astype(jnp.int32)
    return value


def kernel(q, k, v, lengths, g, out, dq, dk, dv,
           kb, vb, s_sc, d_sc, m_sc, dl_sc, acc_q, qt, gt, th, bias,
           gk, gv, mid, side, row, tri,
           f_send, f_recv, c_send, o_send, mid_recv, side_recv, row_recv, h_send, tri_recv):
    me = lax.axis_index("ctx")
    size = lax.axis_size("ctx")
    x = me % 4
    y = (me // 4) % 4
    base = me - x
    right, left = base + (x + 1) % 4, base + (x + 3) % 4
    stores = (kb, vb)

    def slot(kk, j, col):
        return (4 * kk + j - 4 * ((col + j) // 4) + SLOTS) % SLOTS

    def mine(kk, j):
        return slot(kk, j, (x + 4 - j) % 4)

    def remote(src, dst, send, recv, ctx):
        return pltpu.make_async_remote_copy(src_ref=src, dst_ref=dst, send_sem=send, recv_sem=recv,
                                            device_id={"ctx": ctx}, device_id_type=MESH)

    def start(*copies):
        for copy in copies:
            copy.start()

    def sent(*copies):
        for copy in copies:
            copy.wait_send()

    barrier = pltpu.get_barrier_semaphore()

    def greet(ctx):
        pl.semaphore_signal(barrier, inc=1, device_id={"ctx": ctx}, device_id_type=MESH)

    greet(right)
    greet(left)
    peers = 2
    for rows in (1, 2, 3):
        for sign in (1, -1):
            ctx = me + sign * 4 * rows
            on = (ctx >= 0) & (ctx < size)
            if rows == 3:
                on = on & (x <= 1)
            pl.when(on)(lambda ctx=ctx: greet(ctx))
            peers = peers + on.astype(jnp.int32)
    pl.semaphore_wait(barrier, peers)

    def column_copy(n, kk):
        src = (k, v)[n]
        return remote(src, stores[n].at[4 * kk], c_send.at[n, kk - 1], f_recv.at[n, 4 * kk], me + 4 * kk)

    def relay_copy(n):
        return remote(stores[n].at[4], stores[n].at[8], c_send.at[n, 2], f_recv.at[n, 8], me + 4)

    def far_copy(n, d):
        return remote(stores[n].at[d + 3], stores[n].at[d], c_send.at[n, d - 6], f_recv.at[n, d], me + 12)

    def row_copies(n, kk):
        buf = stores[n]
        copies = []
        for side_no, (j, ctx) in enumerate(((1, right), (3, left))):
            to = slot(kk, j, x)
            copies.append(remote(buf.at[4 * kk], buf.at[to], f_send.at[n, kk, side_no], f_recv.at[n, to], ctx))
        return copies

    def onward_copy(n, kk):
        buf, j, ctx = ((kb, 1, right), (vb, 3, left))[n]
        col = (x + 4 - j) % 4
        to = slot(kk, 2, col)
        return remote(buf.at[slot(kk, j, col)], buf.at[to], f_send.at[n, kk, 2], f_recv.at[n, to], ctx)

    def arrived(n, at):
        buf = stores[n]
        remote(buf.at[at], buf.at[at], f_send.at[n, 0, 0], f_recv.at[n, at], right).wait_recv()

    down = [(me + 4 < size), (me + 8 < size) & (y != 3), y == 0,
            (x == 0) & (me + 12 < size), (x <= 1) & (me + 12 < size)]

    @pl.when(down[0])
    def _():
        start(column_copy(0, 1), column_copy(1, 1))

    @pl.when(down[1])
    def _():
        start(column_copy(0, 2), column_copy(1, 2))

    kb[0] = k[...]
    vb[0] = v[...]
    start(*row_copies(0, 0), *row_copies(1, 0))

    for on, d in ((me < 4, 4), (me < 4, 8), ((me < 12) & (x == 0), 9), ((me < 12) & (x <= 1), 10)):
        @pl.when(on)
        def _():
            kb[d] = jnp.zeros((TOK, DIM), BF16)
            vb[d] = jnp.zeros((TOK, DIM), BF16)

    first = jnp.full((TOK, DIM), -1, jnp.int32) * (me * TOK)
    token = lax.broadcasted_iota(jnp.int32, (TOK, DIM), 0)
    end = -me * TOK
    for doc in range(lengths.shape[0]):
        end = end + lengths[doc]
        first = jnp.where(token >= end, end, first)
    th[...] = first
    for h in range(HEADS):
        cols = slice(h * DIM, (h + 1) * DIM)
        qt[h] = q[:, cols].T
        gt[h] = g[:, cols].T
    m_sc[...] = jnp.full_like(m_sc, NEG)

    def scores(d):
        key_at = lax.broadcasted_iota(jnp.int32, (TOK, DIM), 1) - d * TOK
        query_at = lax.broadcasted_iota(jnp.int32, (TOK, DIM), 0)
        for part in (0, 1):
            at = key_at + part * DIM
            seen = (at >= th[...]) & (at <= query_at)
            bias[:, part * DIM:(part + 1) * DIM] = jnp.where(seen, 0.0, NEG)
        key, value = kb[d], vb[d]
        for h in range(HEADS):
            cols = slice(h * DIM, (h + 1) * DIM)
            s = dot_nt(q[:, cols], key) + bias[...]
            s_sc[h, d] = s
            m_sc[h] = jnp.maximum(m_sc[h], jnp.maximum(s[:, :DIM], s[:, DIM:]))
            d_sc[h, d] = dot_nt(g[:, cols], value)

    def valid(kk, j):
        wraps = (j > x).astype(jnp.int32)
        d = 4 * kk + j - 4 * wraps
        return (d >= 0) & (d < BLOCKS), d

    def score_all(table):
        def step_of(step, _):
            ok, d = valid(pick(table, 0, step), pick(table, 1, step))

            @pl.when(ok)
            def _():
                scores(d)

            return 0

        lax.fori_loop(0, len(table), step_of, 0)

    score_all(((0, 0),))
    for n, j in ((0, 1), (1, 3)):
        arrived(n, mine(0, j))
        start(onward_copy(n, 0))
    for n in (0, 1):
        pl.when(me >= 4)(lambda: arrived(n, 4))
        start(*row_copies(n, 1))
        pl.when(down[2])(lambda: start(relay_copy(n)))
    arrived(1, mine(0, 1))
    arrived(0, mine(0, 3))
    pl.when(down[3])(lambda: start(far_copy(0, 9), far_copy(1, 9)))
    score_all(((1, 0), (0, 1)))
    for n in (0, 1):
        pl.when(me >= 4)(lambda: arrived(n, 8))
        start(*row_copies(n, 2))
    arrived(0, mine(0, 2))
    arrived(1, mine(0, 2))
    pl.when(down[4])(lambda: start(far_copy(0, 10), far_copy(1, 10)))
    score_all(((0, 3), (0, 2)))
    for n, j in ((0, 1), (1, 3)):
        arrived(n, mine(1, j))
        start(onward_copy(n, 1))
    arrived(1, mine(1, 1))
    arrived(0, mine(1, 3))
    score_all(((2, 0), (1, 1), (1, 3)))
    for n, j in ((0, 1), (1, 3)):
        arrived(n, mine(2, j))
        start(onward_copy(n, 2))
    arrived(1, mine(2, 1))
    arrived(0, mine(2, 3))
    arrived(0, mine(1, 2))
    arrived(1, mine(1, 2))
    score_all(((1, 2), (2, 1), (2, 3)))
    for d in (9, 10):
        @pl.when((me >= 12) & (x <= d - 9))
        def _():
            arrived(0, d)
            arrived(1, d)
    arrived(0, mine(2, 2))
    arrived(1, mine(2, 2))
    score_all(((3, 1), (3, 2), (2, 2)))

    def finish_head(h, _):
        m = jnp.max(m_sc[h], axis=1, keepdims=True)
        total = jnp.zeros((TOK, 2 * DIM), F32)
        ones = jnp.ones((TOK, DIM), BF16)
        for d in range(BLOCKS):
            p = jnp.exp2((s_sc[h, d] - m) * EXP2).astype(BF16)
            total = total + dot_nn(p, jnp.concatenate([vb[d], ones], 1))
        norm = total[:, DIM:]
        full = total[:, :DIM] / norm
        acc_q[h] = full
        m_sc[h] = m * EXP2 + jnp.log2(norm)
        return 0

    lax.fori_loop(0, HEADS, finish_head, 0)
    for h in range(HEADS):
        cols = slice(h * DIM, (h + 1) * DIM)
        full = acc_q[h]
        out[:, cols] = full.astype(BF16)
        delta = jnp.sum(full * g[:, cols].astype(F32), axis=1, keepdims=True)
        dl_sc[h] = jnp.broadcast_to(delta, (TOK, DIM))
    acc_q[...] = jnp.zeros_like(acc_q)

    def gradients(d):
        key = kb[d]
        key_part = value_part = None
        for h in range(HEADS):
            lse, delta = m_sc[h], dl_sc[h]
            p = jnp.exp2(s_sc[h, d] * EXP2 - jnp.concatenate([lse, lse], 1))
            ds = (p * (d_sc[h, d] - jnp.concatenate([delta, delta], 1))).astype(BF16)
            acc_q[h] += dot_nn(ds, key)
            a, b = dot_nn(qt[h], ds), dot_nn(gt[h], p.astype(BF16))
            key_part = a if h == 0 else key_part + a
            value_part = b if h == 0 else value_part + b
        gk[d] = key_part.astype(BF16)
        gv[d] = value_part.astype(BF16)

    grads = (gk, gv)

    def add(ref, at, *others):
        total = ref[at].astype(F32)
        for other in others:
            total = total + other.astype(F32)
        ref[at] = total.astype(BF16)

    def mid_copy(n, kk):
        return remote(grads[n].at[mine(kk, 2)], mid.at[n, kk], o_send.at[n, kk, 2], mid_recv.at[n, kk], (left, right)[n])

    def side_copy(n, kk, side_no):
        at, ctx = mine(kk, (1, 3)[side_no]), (left, right)[side_no]
        return remote(grads[n].at[at], side.at[n, kk, side_no], o_send.at[n, kk, side_no],
                      side_recv.at[n, kk, side_no], ctx)

    def home_copy(n, kk):
        return remote(grads[n].at[4 * kk], row.at[n, kk - 1], h_send.at[n, kk - 1], row_recv.at[n, kk - 1], me - 4 * kk)

    def tri_copy(n, d):
        return remote(grads[n].at[d], tri.at[n, d - 9], h_send.at[n, d - 7], tri_recv.at[n, d - 9], me - 12)

    def gradients_all(table):
        def step_of(step, _):
            kk, j = pick(table, 0, step), pick(table, 1, step)
            ok, d = valid(kk, j)
            there = (d + SLOTS) % SLOTS

            @pl.when(ok)
            def _():
                gradients(d)

            @pl.when(jnp.logical_not(ok) & (kk < 3))
            def _():
                gk[there] = jnp.zeros((DIM, TOK), BF16)
                gv[there] = jnp.zeros((DIM, TOK), BF16)

            return 0

        lax.fori_loop(0, len(table), step_of, 0)

    def pass_sides(kk):
        for n, j in ((0, 1), (1, 3)):
            mid_copy(n, kk).wait_recv()
            add(grads[n], mine(kk, j), mid[n, kk])
        start(side_copy(0, kk, 0), side_copy(1, kk, 0), side_copy(0, kk, 1), side_copy(1, kk, 1))

    def take_sides(kk):
        for n in (0, 1):
            side_copy(n, kk, 0).wait_recv()
            side_copy(n, kk, 1).wait_recv()
            add(grads[n], 4 * kk, side[n, kk, 0], side[n, kk, 1])
        if kk:
            pl.when(me >= 4 * kk)(lambda: start(home_copy(0, kk), home_copy(1, kk)))

    gradients_all(((3, 2), (3, 1)))
    for d in (10, 9):
        pl.when((me >= 12) & (x <= d - 9))(lambda: start(tri_copy(0, d), tri_copy(1, d)))
    gradients_all(((2, 2),))
    start(mid_copy(0, 2), mid_copy(1, 2))
    gradients_all(((2, 1), (2, 3), (1, 2)))
    start(mid_copy(0, 1), mid_copy(1, 1))
    gradients_all(((2, 0),))
    pass_sides(2)
    gradients_all(((1, 1), (1, 3)))
    pass_sides(1)
    gradients_all(((1, 0), (0, 2)))
    for d in (10, 9):
        if d == 9:
            take_sides(2)
            gradients_all(((0, 1), (0, 3)))

        @pl.when((me + 12 < size) & (x <= d - 9))
        def _():
            for n in (0, 1):
                tri_copy(n, d).wait_recv()
                grads[n][d + 3] = tri[n, d - 9]

        if d == 10:
            start(mid_copy(0, 0), mid_copy(1, 0))
    pass_sides(0)
    gradients_all(((0, 0),))
    take_sides(1)

    for h in range(HEADS):
        dq[:, h * DIM:(h + 1) * DIM] = (acc_q[h] * FACTOR).astype(BF16)
    take_sides(0)
    for kk in (1, 2):
        @pl.when(me + 4 * kk < size)
        def _():
            for n in (0, 1):
                home_copy(n, kk).wait_recv()
                add(grads[n], 0, row[n, kk - 1])
    dk[...] = (gk[0].astype(F32) * FACTOR).T
    dv[...] = gv[0].astype(F32).T

    for n in (0, 1):
        for at, copy in enumerate((column_copy(n, 1), column_copy(n, 2), relay_copy(n), far_copy(n, 9), far_copy(n, 10))):
            pl.when(down[at])(lambda: sent(copy))
        for kk in (0, 1, 2):
            sent(*row_copies(n, kk), onward_copy(n, kk), mid_copy(n, kk), side_copy(n, kk, 0), side_copy(n, kk, 1))
        for kk in (1, 2):
            pl.when(me >= 4 * kk)(lambda: sent(home_copy(n, kk)))
        for d in (9, 10):
            pl.when((me >= 12) & (x <= d - 9))(lambda: sent(tri_copy(n, d)))


def body(queries, keys, values, lengths, output_gradient):
    vmem = pl.BlockSpec(memory_space=pltpu.VMEM)
    wide = (TOK, HEADS * DIM)
    dma = pltpu.SemaphoreType.DMA
    out, dq, dk, dv = pl.pallas_call(
        kernel,
        out_shape=[
            jax.ShapeDtypeStruct(wide, BF16),
            jax.ShapeDtypeStruct(wide, BF16),
            jax.ShapeDtypeStruct((TOK, DIM), F32),
            jax.ShapeDtypeStruct((TOK, DIM), F32),
        ],
        in_specs=[vmem, vmem, vmem, pl.BlockSpec(memory_space=pltpu.SMEM), vmem],
        out_specs=[vmem] * 4,
        scratch_shapes=[
            pltpu.VMEM((SLOTS, TOK, DIM), BF16),
            pltpu.VMEM((SLOTS, TOK, DIM), BF16),
            pltpu.VMEM((HEADS, BLOCKS, TOK, TOK), F32),
            pltpu.VMEM((HEADS, BLOCKS, TOK, TOK), F32),
            pltpu.VMEM((HEADS, TOK, DIM), F32),
            pltpu.VMEM((HEADS, TOK, DIM), F32),
            pltpu.VMEM((HEADS, TOK, DIM), F32),
            pltpu.VMEM((HEADS, DIM, TOK), BF16),
            pltpu.VMEM((HEADS, DIM, TOK), BF16),
            pltpu.VMEM((TOK, DIM), jnp.int32),
            pltpu.VMEM((TOK, TOK), F32),
            pltpu.VMEM((SLOTS, DIM, TOK), BF16),
            pltpu.VMEM((SLOTS, DIM, TOK), BF16),
            pltpu.VMEM((2, 3, DIM, TOK), BF16),
            pltpu.VMEM((2, 3, 2, DIM, TOK), BF16),
            pltpu.VMEM((2, 2, DIM, TOK), BF16),
            pltpu.VMEM((2, 2, DIM, TOK), BF16),
            dma((2, 3, 3)),
            dma((2, SLOTS)),
            dma((2, 5)),
            dma((2, 3, 3)),
            dma((2, 3)),
            dma((2, 3, 2)),
            dma((2, 2)),
            dma((2, 4)),
            dma((2, 2)),
        ],
        compiler_params=pltpu.CompilerParams(
            collective_id=0, has_side_effects=True, vmem_limit_bytes=62 << 20
        ),
    )(queries, keys, values, lengths, output_gradient)
    return out, dq.astype(F32), dk, dv


def solution(mesh):
    spec = P("ctx", "head")
    return jax.shard_map(
        body,
        mesh=mesh,
        in_specs=(spec, spec, spec, P(), spec),
        out_specs=(spec, spec, spec, spec),
        check_vma=False,
    )
```

time: 91 us -> 69.6 us (0.76)
  the two profiles are of different devices: /device:TPU:32 before, /device:TPU:88 now
where the time goes in v2:
time: 69.6 us; the launch traced here: 69.4 us
  Pallas kernels  64 us (92%)
  local copies, waits for them, and re-layouts  2.63 us (4%)
  other arithmetic  2.18 us (3%)
    pallas_call x1, Pallas kernels, body(): pl.pallas_call(kernel, out_shape=[jax.ShapeDtypeStruct(wide, BF16), jax.S...  64 us
    unnamed x9, local copies, waits for them, and re-layouts  2.63 us
    convert_element_type x1, other arithmetic, body(): return (out, dq.astype(F32), dk, dv)  2.18 us

profile of v2, /device:TPU:88, one launch (start us, length us, event | category | flops | bytes accessed | tf_op | source)
XLA Modules:
  0.0 69.4 jit_solution(8778209386519558620)
XLA Ops:
  0.6 64.0 %shard_map.84 = (bf16[256,1024]{1,0:T(8,128)(2,1)}, bf16[256,1024]{1,0:T(8,128)(2,1)}, f32[256,128]{1,0:T(8,128)}, f32[256,128]{1,0:T(8,128)}) custom-call(bf16[256,1024]{1,0:T(8,128)(2,1)} %q.1, bf16[256,128]{1,0:T(8,128)(2,1)} %k.1, bf16[256,128]{1,0:T(8,128)(2,1)} %v.1, s32[32]{0:T(128)} %lengths.1, bf16[256,1024]{1,0:T(8,128)(2,1)} %g.1), custom_call_target="tpu_custom_call" | custom-call | tf_op jit(solution)/shard_map/pallas_call | solution.py:367
  64.6 0.0 copy-start
  64.6 2.2 %convert_element_type.3 = f32[256,1024]{1,0:T(8,128)} convert(bf16[256,1024]{1,0:T(8,128)(2,1)} %get-tuple-element.9) | non-fusion elementwise | flops 262144 | bytes 1572864 | tf_op jit(solution)/shard_map/convert_element_type | solution.py:409
  66.8 0.0 copy-done
  66.8 0.0 copy-start.2
  66.8 0.8 %copy.12 = bf16[256,1024]{1,0:T(8,128)(2,1)} copy(bf16[256,1024]{1,0:T(8,128)(2,1)S(1)} %copy-done) | data formatting | bytes 1048576
  67.6 0.2 copy-done.2
  67.8 0.0 copy-start.1
  67.8 0.7 copy.13
  68.5 0.3 copy-done.1
  68.8 0.7 copy.14
Async XLA Ops:
  64.6 2.2 %copy-start = (bf16[256,1024]{1,0:T(8,128)(2,1)S(1)}, bf16[256,1024]{1,0:T(8,128)(2,1)}, u32[]{:S(2)}) copy-start(bf16[256,1024]{1,0:T(8,128)(2,1)} %get-tuple-element.16) | copy-start | bytes 1572868
  66.8 1.0 %copy-start.2 = (f32[256,128]{1,0:T(8,128)S(1)}, f32[256,128]{1,0:T(8,128)}, u32[]{:S(2)}) copy-start(f32[256,128]{1,0:T(8,128)} %get-tuple-element.18) | copy-start | bytes 393220
  67.8 1.0 %copy-start.1 = (f32[256,128]{1,0:T(8,128)S(1)}, f32[256,128]{1,0:T(8,128)}, u32[]{:S(2)}) copy-start(f32[256,128]{1,0:T(8,128)} %get-tuple-element.19) | copy-start | bytes 393220

commit v3 on v2

--- a/solution.py
+++ b/solution.py
@@ -313,29 +313,31 @@
         pl.when((me >= 12) & (x <= d - 9))(lambda: start(tri_copy(0, d), tri_copy(1, d)))
     gradients_all(((2, 2),))
     start(mid_copy(0, 2), mid_copy(1, 2))
-    gradients_all(((2, 1), (2, 3), (1, 2)))
+    gradients_all(((1, 2),))
     start(mid_copy(0, 1), mid_copy(1, 1))
-    gradients_all(((2, 0),))
+    gradients_all(((2, 1), (2, 3)))
     pass_sides(2)
     gradients_all(((1, 1), (1, 3)))
     pass_sides(1)
-    gradients_all(((1, 0), (0, 2)))
-    for d in (10, 9):
-        if d == 9:
-            take_sides(2)
-            gradients_all(((0, 1), (0, 3)))
-
-        @pl.when((me + 12 < size) & (x <= d - 9))
-        def _():
-            for n in (0, 1):
-                tri_copy(n, d).wait_recv()
-                grads[n][d + 3] = tri[n, d - 9]
-
-        if d == 10:
-            start(mid_copy(0, 0), mid_copy(1, 0))
+    gradients_all(((0, 2), (2, 0), (1, 0), (0, 1), (0, 3), (0, 0)))
+    take_sides(2)
+
+    @pl.when((me + 12 < size) & (x <= 1))
+    def _():
+        for n in (0, 1):
+            tri_copy(n, 10).wait_recv()
+            grads[n][13] = tri[n, 1]
+
+    start(mid_copy(0, 0), mid_copy(1, 0))
+    take_sides(1)
+
+    @pl.when((me + 12 < size) & (x <= 0))
+    def _():
+        for n in (0, 1):
+            tri_copy(n, 9).wait_recv()
+            grads[n][12] = tri[n, 0]
+
     pass_sides(0)
-    gradients_all(((0, 0),))
-    take_sides(1)
 
     for h in range(HEADS):
         dq[:, h * DIM:(h + 1) * DIM] = (acc_q[h] * FACTOR).astype(BF16)
@@ -345,9 +347,14 @@
         def _():
             for n in (0, 1):
                 home_copy(n, kk).wait_recv()
-                add(grads[n], 0, row[n, kk - 1])
-    dk[...] = (gk[0].astype(F32) * FACTOR).T
-    dv[...] = gv[0].astype(F32).T
+
+        @pl.when(me + 4 * kk >= size)
+        def _():
+            for n in (0, 1):
+                row[n, kk - 1] = jnp.zeros((DIM, TOK), BF16)
+    for n, (to, scale) in enumerate(((dk, FACTOR), (dv, 1.0))):
+        total = grads[n][0].astype(F32) + row[n, 0].astype(F32) + row[n, 1].astype(F32)
+        to[...] = (total * scale).T
 
     for n in (0, 1):
         for at, copy in enumerate((column_copy(n, 1), column_copy(n, 2), relay_copy(n), far_copy(n, 9), far_copy(n, 10))):
@@ -358,6 +365,13 @@
             pl.when(me >= 4 * kk)(lambda: sent(home_copy(n, kk)))
         for d in (9, 10):
             pl.when((me >= 12) & (x <= d - 9))(lambda: sent(tri_copy(n, d)))
+
+
+def write_out(out_in, dq_in, dk_in, dv_in, out, dq, dk, dv):
+    out[...] = out_in[...]
+    dq[...] = dq_in[...].astype(F32)
+    dk[...] = dk_in[...]
+    dv[...] = dv_in[...]
 
 
 def body(queries, keys, values, lengths, output_gradient):
@@ -406,7 +420,17 @@
             collective_id=0, has_side_effects=True, vmem_limit_bytes=62 << 20
         ),
     )(queries, keys, values, lengths, output_gradient)
-    return out, dq.astype(F32), dk, dv
+    return pl.pallas_call(
+        write_out,
+        out_shape=[
+            jax.ShapeDtypeStruct(wide, BF16),
+            jax.ShapeDtypeStruct(wide, F32),
+            jax.ShapeDtypeStruct((TOK, DIM), F32),
+            jax.ShapeDtypeStruct((TOK, DIM), F32),
+        ],
+        in_specs=[vmem] * 4,
+        out_specs=[vmem] * 4,
+    )(out, dq, dk, dv)
 
 
 def solution(mesh):

time: 69.6 us -> 67.3 us (0.967)
  local copies, waits for them, and re-layouts: 2.63 us -> 0 us
  Pallas kernels: 64 us -> 66.5 us
  other arithmetic: 2.18 us -> 0 us
    unnamed x9 -> x0, local copies, waits for them, and re-layouts: 2.63 us -> none
    pallas_call x0 -> x1, Pallas kernels: none -> 2.57 us  [body(): pl.pallas_call(write_out, out_shape=[jax.ShapeDtypeStruct(wide, BF16), ja...]
    convert_element_type x1 -> x0, other arithmetic: 2.18 us -> none  [body(): return (out, dq.astype(F32), dk, dv)]
where the time goes in v3:
time: 67.3 us; the launch traced here: 67.1 us
  Pallas kernels  66.5 us (99%)
    pallas_call x1, Pallas kernels, body(): pl.pallas_call(kernel, out_shape=[jax.ShapeDtypeStruct(wide, BF16), jax.S...  63.9 us
    pallas_call x1, Pallas kernels, body(): pl.pallas_call(write_out, out_shape=[jax.ShapeDtypeStruct(wide, BF16), ja...  2.57 us

profile of v3, /device:TPU:88, one launch (start us, length us, event | category | flops | bytes accessed | tf_op | source)
XLA Modules:
  0.0 67.1 jit_solution(16270293272066404473)
XLA Ops:
  0.6 63.9 %shard_map.84 = (bf16[256,1024]{1,0:T(8,128)(2,1)}, bf16[256,1024]{1,0:T(8,128)(2,1)}, f32[256,128]{1,0:T(8,128)}, f32[256,128]{1,0:T(8,128)}) custom-call(bf16[256,1024]{1,0:T(8,128)(2,1)} %q.1, bf16[256,128]{1,0:T(8,128)(2,1)} %k.1, bf16[256,128]{1,0:T(8,128)(2,1)} %v.1, s32[32]{0:T(128)} %lengths.1, bf16[256,1024]{1,0:T(8,128)(2,1)} %g.1), custom_call_target="tpu_custom_call" | custom-call | tf_op jit(solution)/shard_map/pallas_call | solution.py:381
  64.6 2.6 %shard_map.85 = (bf16[256,1024]{1,0:T(8,128)(2,1)}, f32[256,1024]{1,0:T(8,128)}, f32[256,128]{1,0:T(8,128)}, f32[256,128]{1,0:T(8,128)}) custom-call(bf16[256,1024]{1,0:T(8,128)(2,1)} %get-tuple-element.8.out_in, bf16[256,1024]{1,0:T(8,128)(2,1)} %get-tuple-element.9.dq_in, f32[256,128]{1,0:T(8,128)} %get-tuple-element.10.dk_in, ...), custom_call_target="tpu_custom_call" | custom-call | tf_op jit(solution)/shard_map/pallas_call | solution.py:423

commit v4 on v3

--- a/solution.py
+++ b/solution.py
@@ -230,7 +230,12 @@
         m_sc[h] = m * EXP2 + jnp.log2(norm)
         return 0
 
-    lax.fori_loop(0, HEADS, finish_head, 0)
+    def finish_pair(i, _):
+        finish_head(2 * i, 0)
+        finish_head(2 * i + 1, 0)
+        return 0
+
+    lax.fori_loop(0, HEADS // 2, finish_pair, 0)
     for h in range(HEADS):
         cols = slice(h * DIM, (h + 1) * DIM)
         full = acc_q[h]
@@ -295,21 +300,22 @@
         lax.fori_loop(0, len(table), step_of, 0)
 
     def pass_sides(kk):
+        start(side_copy(1, kk, 0), side_copy(0, kk, 1))
         for n, j in ((0, 1), (1, 3)):
             mid_copy(n, kk).wait_recv()
             add(grads[n], mine(kk, j), mid[n, kk])
-        start(side_copy(0, kk, 0), side_copy(1, kk, 0), side_copy(0, kk, 1), side_copy(1, kk, 1))
+            start(side_copy(n, kk, n))
 
     def take_sides(kk):
         for n in (0, 1):
             side_copy(n, kk, 0).wait_recv()
             side_copy(n, kk, 1).wait_recv()
             add(grads[n], 4 * kk, side[n, kk, 0], side[n, kk, 1])
-        if kk:
-            pl.when(me >= 4 * kk)(lambda: start(home_copy(0, kk), home_copy(1, kk)))
-
-    gradients_all(((3, 2), (3, 1)))
-    for d in (10, 9):
+            if kk:
+                pl.when(me >= 4 * kk)(lambda: start(home_copy(n, kk)))
+
+    for d, block in ((10, (3, 2)), (9, (3, 1))):
+        gradients_all((block,))
         pl.when((me >= 12) & (x <= d - 9))(lambda: start(tri_copy(0, d), tri_copy(1, d)))
     gradients_all(((2, 2),))
     start(mid_copy(0, 2), mid_copy(1, 2))

time: 67.3 us -> 65.6 us (0.975)
  Pallas kernels: 66.5 us -> 64.8 us
    pallas_call x1, Pallas kernels: 63.9 us -> 62.2 us  [body(): pl.pallas_call(kernel, out_shape=[jax.ShapeDtypeStruct(wide, BF16), jax.S...]
where the time goes in v4:
time: 65.6 us; the launch traced here: 65.4 us
  Pallas kernels  64.8 us (99%)
    pallas_call x1, Pallas kernels, body(): pl.pallas_call(kernel, out_shape=[jax.ShapeDtypeStruct(wide, BF16), jax.S...  62.2 us
    pallas_call x1, Pallas kernels, body(): pl.pallas_call(write_out, out_shape=[jax.ShapeDtypeStruct(wide, BF16), ja...  2.57 us

profile of v4, /device:TPU:88, one launch (start us, length us, event | category | flops | bytes accessed | tf_op | source)
XLA Modules:
  0.0 65.4 jit_solution(2933279920446739566)
XLA Ops:
  0.6 62.2 %shard_map.84 = (bf16[256,1024]{1,0:T(8,128)(2,1)}, bf16[256,1024]{1,0:T(8,128)(2,1)}, f32[256,128]{1,0:T(8,128)}, f32[256,128]{1,0:T(8,128)}) custom-call(bf16[256,1024]{1,0:T(8,128)(2,1)} %q.1, bf16[256,128]{1,0:T(8,128)(2,1)} %k.1, bf16[256,128]{1,0:T(8,128)(2,1)} %v.1, s32[32]{0:T(128)} %lengths.1, bf16[256,1024]{1,0:T(8,128)(2,1)} %g.1), custom_call_target="tpu_custom_call" | custom-call | tf_op jit(solution)/shard_map/pallas_call | solution.py:387
  62.9 2.6 %shard_map.85 = (bf16[256,1024]{1,0:T(8,128)(2,1)}, f32[256,1024]{1,0:T(8,128)}, f32[256,128]{1,0:T(8,128)}, f32[256,128]{1,0:T(8,128)}) custom-call(bf16[256,1024]{1,0:T(8,128)(2,1)} %get-tuple-element.8.out_in, bf16[256,1024]{1,0:T(8,128)(2,1)} %get-tuple-element.9.dq_in, f32[256,128]{1,0:T(8,128)} %get-tuple-element.10.dk_in, ...), custom_call_target="tpu_custom_call" | custom-call | tf_op jit(solution)/shard_map/pallas_call | solution.py:429

commit v5 on v4

--- a/solution.py
+++ b/solution.py
@@ -33,7 +33,8 @@
     return value
 
 
-def kernel(q, k, v, lengths, g, out, dq, dk, dv,
+def kernel(q_in, k, v, lengths, g_in, out, dq, dk, dv,
+           q, g, load_sem,
            kb, vb, s_sc, d_sc, m_sc, dl_sc, acc_q, qt, gt, th, bias,
            gk, gv, mid, side, row, tri,
            f_send, f_recv, c_send, o_send, mid_recv, side_recv, row_recv, h_send, tri_recv):
@@ -63,6 +64,7 @@
         for copy in copies:
             copy.wait_send()
 
+    loads = [pltpu.make_async_copy(q_in, q, load_sem.at[0]), pltpu.make_async_copy(g_in, g, load_sem.at[1])]
     barrier = pltpu.get_barrier_semaphore()
 
     def greet(ctx):
@@ -79,6 +81,7 @@
                 on = on & (x <= 1)
             pl.when(on)(lambda ctx=ctx: greet(ctx))
             peers = peers + on.astype(jnp.int32)
+    start(*loads)
     pl.semaphore_wait(barrier, peers)
 
     def column_copy(n, kk):
@@ -129,6 +132,9 @@
         def _():
             kb[d] = jnp.zeros((TOK, DIM), BF16)
             vb[d] = jnp.zeros((TOK, DIM), BF16)
+
+    for load in loads:
+        load.wait()
 
     first = jnp.full((TOK, DIM), -1, jnp.int32) * (me * TOK)
     token = lax.broadcasted_iota(jnp.int32, (TOK, DIM), 0)
@@ -382,6 +388,7 @@
 
 def body(queries, keys, values, lengths, output_gradient):
     vmem = pl.BlockSpec(memory_space=pltpu.VMEM)
+    whole = pl.BlockSpec(memory_space=pl.ANY)
     wide = (TOK, HEADS * DIM)
     dma = pltpu.SemaphoreType.DMA
     out, dq, dk, dv = pl.pallas_call(
@@ -392,9 +399,12 @@
             jax.ShapeDtypeStruct((TOK, DIM), F32),
             jax.ShapeDtypeStruct((TOK, DIM), F32),
         ],
-        in_specs=[vmem, vmem, vmem, pl.BlockSpec(memory_space=pltpu.SMEM), vmem],
+        in_specs=[whole, vmem, vmem, pl.BlockSpec(memory_space=pltpu.SMEM), whole],
         out_specs=[vmem] * 4,
         scratch_shapes=[
+            pltpu.VMEM(wide, BF16),
+            pltpu.VMEM(wide, BF16),
+            dma((2,)),
             pltpu.VMEM((SLOTS, TOK, DIM), BF16),
             pltpu.VMEM((SLOTS, TOK, DIM), BF16),
             pltpu.VMEM((HEADS, BLOCKS, TOK, TOK), F32),

time: 65.6 us -> 65.2 us (level)
  no operation moved by 1% of the time
where the time goes in v5:
time: 65.2 us; the launch traced here: 65.1 us
  Pallas kernels  64.4 us (99%)
    pallas_call x1, Pallas kernels, body(): pl.pallas_call(kernel, out_shape=[jax.ShapeDtypeStruct(wide, BF16), jax.S...  61.9 us
    pallas_call x1, Pallas kernels, body(): pl.pallas_call(write_out, out_shape=[jax.ShapeDtypeStruct(wide, BF16), ja...  2.57 us

profile of v5, /device:TPU:88, one launch (start us, length us, event | category | flops | bytes accessed | tf_op | source)
XLA Modules:
  0.0 65.1 jit_solution(12901073360212960766)
XLA Ops:
  0.6 61.9 %shard_map.84 = (bf16[256,1024]{1,0:T(8,128)(2,1)}, bf16[256,1024]{1,0:T(8,128)(2,1)}, f32[256,128]{1,0:T(8,128)}, f32[256,128]{1,0:T(8,128)}) custom-call(bf16[256,1024]{1,0:T(8,128)(2,1)} %q_in.1, bf16[256,128]{1,0:T(8,128)(2,1)} %k.1, bf16[256,128]{1,0:T(8,128)(2,1)} %v.1, s32[32]{0:T(128)} %lengths.1, bf16[256,1024]{1,0:T(8,128)(2,1)} %g_in.1), custom_call_target="tpu_custom_call" | custom-call | tf_op jit(solution)/shard_map/pallas_call | solution.py:394
  62.5 2.6 %shard_map.85 = (bf16[256,1024]{1,0:T(8,128)(2,1)}, f32[256,1024]{1,0:T(8,128)}, f32[256,128]{1,0:T(8,128)}, f32[256,128]{1,0:T(8,128)}) custom-call(bf16[256,1024]{1,0:T(8,128)(2,1)} %get-tuple-element.8.out_in, bf16[256,1024]{1,0:T(8,128)(2,1)} %get-tuple-element.9.dq_in, f32[256,128]{1,0:T(8,128)} %get-tuple-element.10.dk_in, ...), custom_call_target="tpu_custom_call" | custom-call | tf_op jit(solution)/shard_map/pallas_call | solution.py:439
